TPU v7x, 32 devices: a whole 2x2x4 slice. The times are simulated.
32 devices in a mesh: island: 8 (over z, x), fsdp: 4 (over y, core).
Axes of the slice: x: 2, y: 2, z: 4, core: 2. Of those that a mesh axis runs over, the one named last changes fastest.
Arguments:
- pseudo_grad: bfloat16 [8, 8192, 512], P('island', 'fsdp'), may hold values from -40 to 40
- error_buf: bfloat16 [8, 8192, 512], P('island', 'fsdp'), may hold values from -2 to 2
- params: bfloat16 [8192, 512], P('fsdp'), may hold values from -6 to 6
- momentum: float32 [8, 12288], P('island', 'fsdp'), may hold values from -4 to 4
- sel_blocks: int32 [8, 512], P('island', 'fsdp'), may hold values from 0 to 255, as said below
- coef_index: int32 [1024, 64], P('fsdp'), may hold values from 0 to 4095, as said below
- owner_map: int32 [1024], P('fsdp'), may hold values from 0 to 7, as said below
Outputs:
- new_params: bfloat16 [8192, 512], P('fsdp')
- new_error: bfloat16 [8, 8192, 512], P('island', 'fsdp')
- new_momentum: float32 [8, 12288], P('island', 'fsdp')
Inputs may be any that keep to these rules, and one draw needn't show every extreme that they name: `sel_blocks`: each island's 128 entries for one shard are distinct blocks of that shard. `coef_index`: each row holds 64 distinct positions. `owner_map`: within each shard of 256 blocks an island owns at most 48 blocks, and some island owns exactly 48.
All inputs are finite; a program needn't handle non-finite values.
Results may differ from a plain program's by a relative error of at most 0.0032.
Values may be sent and summed in bfloat16 or wider, within the bound.
A program may use at most 64 MiB of HBM per device.

v0:
```python
import functools

import numpy as np

import jax
import jax.numpy as jnp
from jax import lax
from jax.experimental import pallas as pl
from jax.experimental.pallas import tpu as pltpu
from jax.sharding import PartitionSpec as P

BETA_FACTOR = 0.9
OUTER_RATE = 0.5
EPSILON = 1e-06
precise_mode = lax.Precision.HIGHEST


def cosine_table():
    freqs = jnp.arange(64, dtype=jnp.float32)[:, None]
    points = jnp.arange(64, dtype=jnp.float32)[None, :]
    scaling = jnp.where(freqs == 0.0, jnp.sqrt(1.0 / 64.0), jnp.sqrt(2.0 / 64.0))
    return scaling * jnp.cos(jnp.pi * (2.0 * points + 1.0) * freqs / 128.0)


def to_blocks(field):
    row_blocks = field.shape[0] // 64
    col_blocks = field.shape[1] // 64
    return (
        field.reshape(row_blocks, 64, col_blocks, 64)
        .transpose(0, 2, 1, 3)
        .reshape(row_blocks * col_blocks, 64, 64)
    )


def from_blocks(blocks, row_total, col_total):
    row_blocks = row_total // 64
    col_blocks = col_total // 64
    return (
        blocks.reshape(row_blocks, col_blocks, 64, 64)
        .transpose(0, 2, 1, 3)
        .reshape(row_total, col_total)
    )


def forward_blocks(cosine, blocks):
    return jnp.einsum("ij,bjk,lk->bil", cosine, blocks, cosine, precision=precise_mode)


def inverse_blocks(cosine, blocks):
    return jnp.einsum("ji,bjk,kl->bil", cosine, blocks, cosine, precision=precise_mode)


def scatter_coefs(values, positions):
    amount = values.shape[0]
    return (
        jnp.zeros((amount, 4096), jnp.float32)
        .at[jnp.arange(amount)[:, None], positions]
        .set(values)
    )


def plain_on_device(pseudo_grad, error_buf, params, momentum, sel_blocks, coef_index, owner_map):
    cosine = cosine_table()
    islands = lax.axis_size("island")
    my_island = lax.axis_index("island")
    shard_rows = params.shape[0]
    columns = params.shape[1]
    n_blocks = coef_index.shape[0]
    coef_total = coef_index.shape[1]
    capacity = momentum.shape[1] // coef_total
    summed = pseudo_grad[0].astype(jnp.float32) + error_buf[0].astype(jnp.float32)
    blocks = to_blocks(summed)
    spectra = forward_blocks(cosine, blocks).reshape(n_blocks, 4096)
    picked = jnp.take_along_axis(spectra, coef_index, axis=1)
    chosen = sel_blocks[0]
    block_ids = jnp.arange(n_blocks, dtype=jnp.int32)
    chosen_mask = jnp.any(chosen[:, None] == block_ids[None, :], axis=0).astype(jnp.float32)
    outgoing = picked * chosen_mask[:, None]
    rebuilt = inverse_blocks(cosine, scatter_coefs(outgoing, coef_index).reshape(n_blocks, 64, 64))
    new_error = from_blocks(blocks - rebuilt, shard_rows, columns).astype(jnp.bfloat16)[None]
    earlier = (owner_map[None, :] == owner_map[:, None]) & (block_ids[None, :] < block_ids[:, None])
    slot_of = jnp.sum(earlier.astype(jnp.int32), axis=1)
    target = owner_map * capacity + slot_of
    own_slots = my_island * capacity + jnp.arange(capacity, dtype=jnp.int32)
    owned_mask = target[None, :] == own_slots[:, None]
    owned_ids = jnp.sum(jnp.where(owned_mask, block_ids[None, :], 0), axis=1)
    owned_live = jnp.any(owned_mask, axis=1)
    owned_pattern = jnp.sum(jnp.where(owned_mask[:, :, None], coef_index[None, :, :], 0), axis=1)
    listed = outgoing[chosen]
    piece_values = lax.all_gather(listed, "island", axis=0, tiled=True)
    piece_ids = lax.all_gather(chosen, "island", axis=0, tiled=True)
    matches = ((piece_ids[None, :] == owned_ids[:, None]) & owned_live[:, None]).astype(jnp.float32)
    totals = jnp.dot(matches, piece_values, precision=precise_mode)
    counts = jnp.sum(matches, axis=1)
    average = totals / jnp.maximum(counts, 1.0)[:, None]
    previous = momentum[0].reshape(capacity, coef_total)
    refreshed = BETA_FACTOR * previous + average
    update_coef = average + BETA_FACTOR * refreshed
    new_momentum = refreshed.reshape(1, capacity * coef_total)
    owner_dense = inverse_blocks(
        cosine, scatter_coefs(update_coef, owned_pattern).reshape(capacity, 64, 64)
    )
    owner_dense = owner_dense.reshape(capacity, 4096).astype(jnp.bfloat16)
    gathered_dense = lax.all_gather(owner_dense, "island", axis=0, tiled=True)
    selector = (target[:, None] == jnp.arange(islands * capacity, dtype=jnp.int32)[None, :]).astype(
        jnp.bfloat16
    )
    received = jnp.dot(selector, gathered_dense, preferred_element_type=jnp.float32)
    local_square = jnp.sum(received * received)
    total_square = lax.psum(local_square, "fsdp")
    scale_root = jnp.sqrt(total_square / (shard_rows * lax.axis_size("fsdp") * columns) + EPSILON)
    shifted = from_blocks(received.reshape(n_blocks, 64, 64), shard_rows, columns)
    new_params = (params.astype(jnp.float32) - OUTER_RATE * shifted / scale_root).astype(
        jnp.bfloat16
    )
    return (new_params, new_error, new_momentum)


MESH = pl.DeviceIdType.MESH
TILE = 256
F32 = jnp.float32
BF16 = jnp.bfloat16


def cosine_parts():
    freqs = np.arange(64)[:, None]
    points = np.arange(64)[None, :]
    scaling = np.where(freqs == 0, np.sqrt(1.0 / 64.0), np.sqrt(2.0 / 64.0))
    cosine = scaling * np.cos(np.pi * (2.0 * points + 1.0) * freqs / 128.0)
    diagonal = np.kron(np.eye(4), cosine).astype(np.float32)
    parts = []
    for table in (diagonal, diagonal.T):
        high = table.astype(BF16)
        parts += [high, (table - high.astype(np.float32)).astype(BF16)]
    return np.stack(parts)


def iota(shape, dim):
    return lax.broadcasted_iota(jnp.int32, shape, dim)


def split(value):
    high = value.astype(BF16)
    return high, (value - high.astype(F32)).astype(BF16)


def dot(a, b):
    return jnp.dot(a, b, preferred_element_type=F32)


def exact_dot(a, b, dims):
    return lax.dot_general(
        a, b, (dims, ((), ())), precision=precise_mode, preferred_element_type=F32
    )


def times_table(parts, table):
    rows = parts[0].shape[0]
    both = dot(jnp.concatenate(parts, axis=0), table[0])
    return both[:rows] + both[rows:] + dot(parts[0], table[1])


def table_times(table, parts):
    return dot(table[0], parts[0]) + dot(table[0], parts[1]) + dot(table[1], parts[0])


def unit_masks(positions):
    rows = lax.shift_right_logical(positions, 6)
    cols = (positions & 63) + (iota((1, TILE), 1) & -64)
    row_mask = iota((64, TILE), 0) == rows
    col_mask = jnp.where(iota((TILE, TILE), 0) == cols, 1.0, 0.0).astype(BF16)
    return row_mask, col_mask


def gather_unit(spectrum, positions):
    row_mask, col_mask = unit_masks(positions)
    both = dot(jnp.concatenate(split(spectrum), axis=0), col_mask)
    return jnp.sum(jnp.where(row_mask, both[:64] + both[64:], 0.0), axis=0, keepdims=True)


def scatter_unit(values, positions):
    row_mask, col_mask = unit_masks(positions)
    high, low = split(jnp.where(row_mask, values, 0.0))
    both = lax.dot_general(
        jnp.concatenate([high, low], axis=0),
        col_mask,
        (((1,), (1,)), ((), ())),
        preferred_element_type=F32,
    ).astype(BF16)
    return both[:64], both[64:]


def decode_tile(values, positions, half, forward, backward):
    highs, lows = [], []
    for strip in range(4):
        unit = 2 * strip + half
        high, low = scatter_unit(values[unit : unit + 1], positions[unit : unit + 1])
        highs.append(high)
        lows.append(low)
    parts = (jnp.concatenate(highs, axis=0), jnp.concatenate(lows, axis=0))
    return table_times(backward, split(times_table(parts, forward)))


def kernel(
    n,
    m,
    elements,
    grad_ref,
    err_ref,
    params_ref,
    mom_ref,
    sel_row_ref,
    sel_col_ref,
    index_ref,
    owner_row_ref,
    owner_col_ref,
    table_ref,
    new_params_ref,
    new_err_ref,
    new_mom_ref,
    early,
    early_in,
    sent,
    sent_in,
    coefs,
    update,
    squares,
    squares_in,
    early_send,
    early_recv,
    sent_send,
    sent_recv,
    coefs_send,
    coefs_recv,
    squares_send,
    squares_recv,
):
    me = lax.axis_index("island")
    shard = lax.axis_index("fsdp")
    units, width = index_ref.shape
    slots, kept = mom_ref.shape
    n_blocks = owner_col_ref.shape[0]

    def island_peer(d):
        return lax.rem(me + d, n)

    def island_source(d):
        return lax.rem(me - d + n, n)

    barrier = pltpu.get_barrier_semaphore()
    for d in range(1, n):
        pl.semaphore_signal(barrier, inc=1, device_id=(island_peer(d), shard), device_id_type=MESH)
    for d in range(1, m):
        pl.semaphore_signal(
            barrier, inc=1, device_id=(me, lax.rem(shard + d, m)), device_id_type=MESH
        )
    forward = (table_ref[0], table_ref[1])
    backward = (table_ref[2], table_ref[3])

    in_unit = iota((units, sel_row_ref.shape[1]), 0) == lax.shift_right_logical(sel_row_ref[...], 2)
    lane_block = lax.shift_right_logical(iota((1, width), 1), 6)
    in_lane = (sel_col_ref[...] & 3) == lane_block
    mask = dot(
        jnp.where(in_unit, 1.0, 0.0).astype(BF16), jnp.where(in_lane, 1.0, 0.0).astype(BF16)
    )
    lanes = iota((1, n_blocks), 1)
    block_row = lax.rem(lanes, units) * 4 + lax.div(lanes, units)
    owner_row = owner_row_ref[...]
    earlier = (owner_col_ref[...] == owner_row) & (iota((n_blocks, n_blocks), 0) < block_row)
    slot_row = jnp.sum(jnp.where(earlier, 1, 0), axis=0, keepdims=True)
    held = jnp.where(
        (iota((slots, n_blocks), 0) == slot_row) & (owner_row == me), 1.0, 0.0
    )
    momentum = mom_ref[...]
    previous = jnp.concatenate(
        [
            exact_dot(held[:, j * units : (j + 1) * units], momentum, ((0,), (0,)))
            for j in range(4)
        ],
        axis=1,
    )
    for q in range(n):
        early[q, 0:8] = mask[8 * q : 8 * q + 8]
        early[q, 8:16] = previous[8 * q : 8 * q + 8]

    pl.semaphore_wait(barrier, n + m - 2)

    def early_copy(d):
        return pltpu.make_async_remote_copy(
            src_ref=early.at[island_peer(d)],
            dst_ref=early_in.at[d],
            send_sem=early_send.at[d],
            recv_sem=early_recv.at[d],
            device_id=(island_peer(d), shard),
            device_id_type=MESH,
        )

    def sent_copy(d):
        return pltpu.make_async_remote_copy(
            src_ref=sent.at[island_peer(d)],
            dst_ref=sent_in.at[d],
            send_sem=sent_send.at[d],
            recv_sem=sent_recv.at[d],
            device_id=(island_peer(d), shard),
            device_id_type=MESH,
        )

    def coefs_copy(d, slot):
        return pltpu.make_async_remote_copy(
            src_ref=coefs.at[slot],
            dst_ref=coefs.at[slot],
            send_sem=coefs_send.at[d],
            recv_sem=coefs_recv.at[d],
            device_id=(island_peer(d), shard),
            device_id_type=MESH,
        )

    def squares_copy(d):
        return pltpu.make_async_remote_copy(
            src_ref=squares,
            dst_ref=squares_in.at[d],
            send_sem=squares_send.at[d],
            recv_sem=squares_recv.at[d],
            device_id=(me, lax.rem(shard + d, m)),
            device_id_type=MESH,
        )

    def rows_of(group):
        return pl.ds(pl.multiple_of(group * TILE, TILE), TILE)

    def units_of(group):
        return pl.ds(pl.multiple_of(group * 8, 8), 8)

    def summed(group, half):
        cols = pl.ds(half * TILE, TILE)
        return grad_ref[rows_of(group), cols].astype(F32) + err_ref[rows_of(group), cols].astype(F32)

    @pl.loop(1, n)
    def _(d):
        early_copy(d).start()

    def pick_group(group):
        positions = index_ref[units_of(group), :]
        picked = [None] * 8
        for half in range(2):
            middle = times_table(split(summed(group, half)), backward)
            spectrum = table_times(forward, split(middle))
            for strip in range(4):
                unit = 2 * strip + half
                picked[unit] = gather_unit(
                    spectrum[strip * 64 : strip * 64 + 64], positions[unit : unit + 1]
                )
        sent[group] = jnp.concatenate(picked, axis=0) * early[group, 0:8]

    @pl.loop(1, n)
    def _(d):
        pick_group(island_peer(d))
        sent_copy(d).start()

    pick_group(me)

    def error_group(group):
        positions = index_ref[units_of(group), :]
        values = sent[group]
        for half in range(2):
            rebuilt = decode_tile(values, positions, half, forward, backward)
            new_err_ref[rows_of(group), pl.ds(half * TILE, TILE)] = (
                summed(group, half) - rebuilt
            ).astype(BF16)

    @pl.loop(0, n // 2)
    def _(group):
        error_group(group)

    @pl.loop(1, n)
    def _(d):
        early_copy(d).wait_recv()
        sent_copy(d).wait_recv()

    totals = sent[me]
    counts = early[me, 0:8]
    owned = early[me, 8:16]
    for d in range(1, n):
        totals += sent_in[d]
        counts += early_in[d, 0:8]
        owned += early_in[d, 8:16]
    average = totals / jnp.maximum(counts, 1.0)
    coefs[me] = average + BETA_FACTOR * (BETA_FACTOR * owned + average)

    @pl.loop(1, n)
    def _(d):
        coefs_copy(d, me).start()

    @pl.loop(n // 2, n)
    def _(group):
        error_group(group)

    def update_group(group, total):
        positions = index_ref[units_of(group), :]
        values = coefs[group]
        for half in range(2):
            piece = decode_tile(values, positions, half, forward, backward).astype(BF16)
            update[rows_of(group), pl.ds(half * TILE, TILE)] = piece
            wide = piece.astype(F32)
            total += jnp.sum((wide * wide).reshape(TILE // 8, 8, TILE), axis=0)
        return total

    total = update_group(me, jnp.zeros((8, TILE), F32))

    def arrived(d, total):
        source = island_source(d)
        coefs_copy(d, source).wait_recv()
        return update_group(source, total)

    total = lax.fori_loop(1, n, arrived, total)
    squares[...] = jnp.broadcast_to(jnp.sum(total, keepdims=True), squares.shape)
    for d in range(1, m):
        squares_copy(d).start()

    everything = jnp.concatenate([coefs[q] for q in range(n)], axis=0)
    own = jnp.zeros((slots, kept), F32)
    for j in range(4):
        own += exact_dot(
            held[:, j * units : (j + 1) * units],
            everything[:, j * kept : (j + 1) * kept],
            ((1,), (0,)),
        )
    live = jnp.sum(held, axis=1, keepdims=True)
    own_average = (own - (BETA_FACTOR * BETA_FACTOR) * momentum * live) / (1.0 + BETA_FACTOR)
    new_mom_ref[...] = BETA_FACTOR * momentum + own_average

    for d in range(1, m):
        squares_copy(d).wait_recv()
    total_square = squares[...]
    for d in range(1, m):
        total_square += squares_in[d]
    step = OUTER_RATE / jnp.sqrt(total_square / elements + EPSILON)
    step = step[0:1, 0:1]

    @pl.loop(0, n)
    def _(group):
        new_params_ref[rows_of(group), :] = (
            params_ref[rows_of(group), :].astype(F32) - update[rows_of(group), :].astype(F32) * step
        ).astype(BF16)

    @pl.loop(1, n)
    def _(d):
        early_copy(d).wait_send()
        sent_copy(d).wait_send()
        coefs_copy(d, me).wait_send()

    for d in range(1, m):
        squares_copy(d).wait_send()


def on_device(pseudo_grad, error_buf, params, momentum, sel_blocks, coef_index, owner_map):
    n = lax.axis_size("island")
    m = lax.axis_size("fsdp")
    rows, columns = params.shape
    n_blocks, kept = coef_index.shape
    units = n_blocks // 4
    if rows != n * TILE or columns != 2 * TILE or kept != 64:
        return plain_on_device(
            pseudo_grad, error_buf, params, momentum, sel_blocks, coef_index, owner_map
        )
    slots = momentum.shape[1] // kept
    chunk = (n, 8, TILE)
    vmem = pl.BlockSpec(memory_space=pltpu.VMEM)
    new_params, new_error, new_momentum = pl.pallas_call(
        functools.partial(kernel, n, m, rows * m * columns),
        out_shape=(
            jax.ShapeDtypeStruct((rows, columns), BF16),
            jax.ShapeDtypeStruct((rows, columns), BF16),
            jax.ShapeDtypeStruct((slots, kept), F32),
        ),
        in_specs=[vmem] * 10,
        out_specs=(vmem, vmem, vmem),
        scratch_shapes=[
            pltpu.VMEM((n, 16, TILE), F32),
            pltpu.VMEM((n, 16, TILE), F32),
            pltpu.VMEM(chunk, F32),
            pltpu.VMEM(chunk, F32),
            pltpu.VMEM(chunk, F32),
            pltpu.VMEM((rows, columns), BF16),
            pltpu.VMEM((8, 128), F32),
            pltpu.VMEM((m, 8, 128), F32),
            pltpu.SemaphoreType.DMA((n,)),
            pltpu.SemaphoreType.DMA((n,)),
            pltpu.SemaphoreType.DMA((n,)),
            pltpu.SemaphoreType.DMA((n,)),
            pltpu.SemaphoreType.DMA((n,)),
            pltpu.SemaphoreType.DMA((n,)),
            pltpu.SemaphoreType.DMA((m,)),
            pltpu.SemaphoreType.DMA((m,)),
        ],
        compiler_params=pltpu.CompilerParams(
            collective_id=0, has_side_effects=True, vmem_limit_bytes=48 * 2**20
        ),
        name="outer_step",
    )(
        pseudo_grad[0],
        error_buf[0],
        params,
        momentum.reshape(slots, kept),
        sel_blocks,
        sel_blocks.reshape(-1, 1),
        coef_index.reshape(units, TILE),
        owner_map.reshape(units, 4).T.reshape(1, n_blocks),
        owner_map.reshape(n_blocks, 1),
        jnp.asarray(cosine_parts()),
    )
    return (new_params, new_error[None], new_momentum.reshape(1, slots * kept))


def solution(mesh):
    in_specs = (
        P("island", "fsdp", None),
        P("island", "fsdp", None),
        P("fsdp", None),
        P("island", "fsdp"),
        P("island", "fsdp"),
        P("fsdp", None),
        P("fsdp"),
    )
    out_specs = (P("fsdp", None), P("island", "fsdp", None), P("island", "fsdp"))
    return jax.shard_map(
        on_device, mesh=mesh, in_specs=in_specs, out_specs=out_specs, check_vma=False
    )
```

profile of v0, /device:TPU:0, one launch (start us, length us, event | category | flops | bytes accessed | tf_op | source)
XLA Modules:
  0.0 65.5 jit_solution(4023060610605912558)
XLA Ops:
  0.6 0.5 broadcast.3
  1.1 1.4 %reduce.3 = f32[3072]{0:T(1024)S(1)} reduce(f32[1,3072]{1,0:T(1,128)} %param.11, f32[]{:T(128)} %broadcast.3), dimensions={0}, to_apply=%param.11.reduce_sub_computation.3 | reduce | bytes 24580 | tf_op args[3]
  2.5 0.1 reshape.27.mom_ref
  2.6 0.8 %reshape.30 = s32[64,4]{1,0:T(8,128)S(1)} reshape(s32[256]{0:T(256)} %param.14) | data formatting | bytes 2048 | tf_op jit(solution)/shard_map/reshape | solution.py:508
  3.4 0.1 copy.14
  3.5 0.1 reshape.31.owner_row_ref
  3.5 0.8 %copy.15.sel_col_ref = s32[128,1]{1,0:T(8,128)S(1)} copy(s32[128,1]{0,1:T(1,128)} %bitcast.7) | data formatting | bytes 1024 | tf_op jit(solution)/shard_map/reshape | solution.py:506
  4.3 0.9 %copy.13 = s32[256,64]{1,0:T(8,128)S(1)} copy(s32[256,64]{0,1:T(8,128)} %param.13) | data formatting | bytes 131072 | tf_op args[5]
  5.2 0.1 reshape.29.index_ref
  5.3 0.8 %copy.16.owner_col_ref = s32[256,1]{1,0:T(8,128)S(1)} copy(s32[256,1]{0,1:T(1,128)} %bitcast.11) | data formatting | bytes 2048 | tf_op jit(solution)/shard_map/reshape | solution.py:509
  6.2 0.0 copy-start.1
  6.2 1.0 %copy-done.1 = bf16[4,256,256]{2,1,0:T(8,128)(2,1)S(1)} copy-done((bf16[4,256,256]{2,1,0:T(8,128)(2,1)S(1)}, bf16[4,256,256]{2,1,0:T(8,128)(2,1)}, u32[]{:S(2)}) %copy-start.1) | copy-done | bytes 524312
  7.2 0.0 copy-start.2
  7.2 0.7 copy-done.2
  7.9 51.3 %outer_step.1 = (bf16[2048,512]{1,0:T(8,128)(2,1)S(1)}, bf16[2048,512]{1,0:T(8,128)(2,1)S(1)}, f32[48,64]{1,0:T(8,128)S(1)}) custom-call(bf16[2048,512]{1,0:T(8,128)(2,1)} %bitcast.8, bf16[2048,512]{1,0:T(8,128)(2,1)} %bitcast.9, bf16[2048,512]{1,0:T(8,128)(2,1)} %params_ref.1, f32[48,64]{1,0:T(8,128)S(1)} %reshape.27.mom_ref, s32[1,128]{1,0:T(1,128)S(1)} %copy-done.2, ...), custom_call_target="tpu_custom_call" | custom-call | tf_op jit(solution)/shard_map/outer_step/pallas_call | solution.py:469
  59.2 0.0 copy-start
  59.2 1.3 %copy-done = bf16[2048,512]{1,0:T(8,128)(2,1)} copy-done((bf16[2048,512]{1,0:T(8,128)(2,1)}, bf16[2048,512]{1,0:T(8,128)(2,1)S(1)}, u32[]{:S(2)}) %copy-start) | copy-done | bytes 2097176
  60.5 0.7 %reshape.33 = f32[1,3072]{1,0:T(1,128)} reshape(f32[48,64]{1,0:T(8,128)S(1)} %get-tuple-element.8) | data formatting | bytes 24576 | tf_op jit(solution)/shard_map/reshape | solution.py:512
  61.2 3.0 %copy.19 = bf16[2048,512]{1,0:T(8,128)(2,1)} copy(bf16[2048,512]{1,0:T(8,128)(2,1)} %copy-done) | data formatting | bytes 4194304
  64.2 1.3 %copy.20 = bf16[1,2048,512]{2,1,0:T(8,128)(2,1)} copy(bf16[1,2048,512]{2,1,0:T(8,128)(2,1)S(1)} %bitcast.6) | data formatting | bytes 4194304
Async XLA Ops:
  6.2 1.0 %copy-start.1 = (bf16[4,256,256]{2,1,0:T(8,128)(2,1)S(1)}, bf16[4,256,256]{2,1,0:T(8,128)(2,1)}, u32[]{:S(2)}) copy-start(bf16[4,256,256]{2,1,0:T(8,128)(2,1)} %constant.2.clone.table_ref) | copy-start | bytes 1572868
  7.2 0.7 copy-start.2
  59.2 1.3 %copy-start = (bf16[2048,512]{1,0:T(8,128)(2,1)}, bf16[2048,512]{1,0:T(8,128)(2,1)S(1)}, u32[]{:S(2)}) copy-start(bf16[2048,512]{1,0:T(8,128)(2,1)S(1)} %get-tuple-element.12) | copy-start | bytes 6291460
where the time goes:
time: 65.9 us; the launch traced here: 65.5 us
  Pallas kernels  51.3 us (78%)
  local copies, waits for them, and re-layouts  12.2 us (19%)
  other arithmetic  1.38 us (2%)
  between operations  0.68 us (1%)
    pallas_call x1, Pallas kernels, on_device(): pl.pallas_call(functools.partial(kernel, n, m, rows * m * columns), out_s...  51.3 us
    unnamed x10, local copies, waits for them, and re-layouts  8.81 us
    unnamed x1, other arithmetic  1.38 us

commit v1 on v0

--- a/solution.py
+++ b/solution.py
@@ -154,51 +154,65 @@
     )
 
 
-def times_table(parts, table):
+def times_table(parts, table_ref, which):
     rows = parts[0].shape[0]
-    both = dot(jnp.concatenate(parts, axis=0), table[0])
-    return both[:rows] + both[rows:] + dot(parts[0], table[1])
-
-
-def table_times(table, parts):
-    return dot(table[0], parts[0]) + dot(table[0], parts[1]) + dot(table[1], parts[0])
-
-
-def unit_masks(positions):
-    rows = lax.shift_right_logical(positions, 6)
+    both = dot(jnp.concatenate(parts, axis=0), table_ref[which])
+    return both[:rows] + both[rows:] + dot(parts[0], table_ref[which + 1])
+
+
+def table_times(table_ref, which, parts):
+    stacked = table_ref[which : which + 2].reshape(2 * TILE, TILE)
+    both = dot(stacked, parts[0])
+    return both[:TILE] + both[TILE:] + dot(table_ref[which], parts[1])
+
+
+def row_mask_of(positions):
+    return iota((64, TILE), 0) == lax.shift_right_logical(positions, 6)
+
+
+def col_mask_of(positions):
     cols = (positions & 63) + (iota((1, TILE), 1) & -64)
-    row_mask = iota((64, TILE), 0) == rows
-    col_mask = jnp.where(iota((TILE, TILE), 0) == cols, 1.0, 0.0).astype(BF16)
-    return row_mask, col_mask
-
-
-def gather_unit(spectrum, positions):
-    row_mask, col_mask = unit_masks(positions)
+    rows = iota((TILE, TILE), 0).astype(F32).astype(BF16)
+    here = rows == cols.astype(F32).astype(BF16)
+    return jnp.where(here, jnp.ones((), BF16), jnp.zeros((), BF16))
+
+
+def gather_unit(spectrum, positions, col_mask):
     both = dot(jnp.concatenate(split(spectrum), axis=0), col_mask)
-    return jnp.sum(jnp.where(row_mask, both[:64] + both[64:], 0.0), axis=0, keepdims=True)
-
-
-def scatter_unit(values, positions):
-    row_mask, col_mask = unit_masks(positions)
-    high, low = split(jnp.where(row_mask, values, 0.0))
-    both = lax.dot_general(
-        jnp.concatenate([high, low], axis=0),
+    return jnp.sum(
+        jnp.where(row_mask_of(positions), both[:64] + both[64:], 0.0), axis=0, keepdims=True
+    )
+
+
+def scatter_unit(parts, col_mask):
+    return lax.dot_general(
+        jnp.concatenate(parts, axis=0),
         col_mask,
         (((1,), (1,)), ((), ())),
         preferred_element_type=F32,
     ).astype(BF16)
-    return both[:64], both[64:]
-
-
-def decode_tile(values, positions, half, forward, backward):
+
+
+def decode_tile(values, positions, masks_ref, first, half, table_ref):
     highs, lows = [], []
     for strip in range(4):
         unit = 2 * strip + half
-        high, low = scatter_unit(values[unit : unit + 1], positions[unit : unit + 1])
-        highs.append(high)
-        lows.append(low)
+        placed = jnp.where(row_mask_of(positions[unit : unit + 1]), values[unit : unit + 1], 0.0)
+        both = scatter_unit(split(placed), masks_ref[first + unit])
+        highs.append(both[:64])
+        lows.append(both[64:])
     parts = (jnp.concatenate(highs, axis=0), jnp.concatenate(lows, axis=0))
-    return table_times(backward, split(times_table(parts, forward)))
+    return table_times(table_ref, 2, split(times_table(parts, table_ref, 0)))
+
+
+def decode_tile_short(values, positions, masks_ref, first, half, table_ref):
+    pieces = []
+    for strip in range(4):
+        unit = 2 * strip + half
+        placed = jnp.where(row_mask_of(positions[unit : unit + 1]), values[unit : unit + 1], 0.0)
+        pieces.append(scatter_unit([placed.astype(BF16)], masks_ref[first + unit]))
+    middle = dot(jnp.concatenate(pieces, axis=0), table_ref[0]).astype(BF16)
+    return dot(table_ref[2], middle)
 
 
 def kernel(
@@ -207,7 +221,6 @@
     elements,
     grad_ref,
     err_ref,
-    params_ref,
     mom_ref,
     sel_row_ref,
     sel_col_ref,
@@ -215,15 +228,16 @@
     owner_row_ref,
     owner_col_ref,
     table_ref,
-    new_params_ref,
+    update,
     new_err_ref,
     new_mom_ref,
+    step_ref,
+    masks,
     early,
     early_in,
     sent,
     sent_in,
     coefs,
-    update,
     squares,
     squares_in,
     early_send,
@@ -254,8 +268,6 @@
         pl.semaphore_signal(
             barrier, inc=1, device_id=(me, lax.rem(shard + d, m)), device_id_type=MESH
         )
-    forward = (table_ref[0], table_ref[1])
-    backward = (table_ref[2], table_ref[3])
 
     in_unit = iota((units, sel_row_ref.shape[1]), 0) == lax.shift_right_logical(sel_row_ref[...], 2)
     lane_block = lax.shift_right_logical(iota((1, width), 1), 6)
@@ -343,12 +355,14 @@
         positions = index_ref[units_of(group), :]
         picked = [None] * 8
         for half in range(2):
-            middle = times_table(split(summed(group, half)), backward)
-            spectrum = table_times(forward, split(middle))
+            middle = times_table(split(summed(group, half)), table_ref, 2)
+            spectrum = table_times(table_ref, 0, split(middle))
             for strip in range(4):
                 unit = 2 * strip + half
+                col_mask = col_mask_of(positions[unit : unit + 1])
+                masks[group * 8 + unit] = col_mask
                 picked[unit] = gather_unit(
-                    spectrum[strip * 64 : strip * 64 + 64], positions[unit : unit + 1]
+                    spectrum[strip * 64 : strip * 64 + 64], positions[unit : unit + 1], col_mask
                 )
         sent[group] = jnp.concatenate(picked, axis=0) * early[group, 0:8]
 
@@ -363,7 +377,7 @@
         positions = index_ref[units_of(group), :]
         values = sent[group]
         for half in range(2):
-            rebuilt = decode_tile(values, positions, half, forward, backward)
+            rebuilt = decode_tile_short(values, positions, masks, group * 8, half, table_ref)
             new_err_ref[rows_of(group), pl.ds(half * TILE, TILE)] = (
                 summed(group, half) - rebuilt
             ).astype(BF16)
@@ -399,7 +413,7 @@
         positions = index_ref[units_of(group), :]
         values = coefs[group]
         for half in range(2):
-            piece = decode_tile(values, positions, half, forward, backward).astype(BF16)
+            piece = decode_tile(values, positions, masks, group * 8, half, table_ref).astype(BF16)
             update[rows_of(group), pl.ds(half * TILE, TILE)] = piece
             wide = piece.astype(F32)
             total += jnp.sum((wide * wide).reshape(TILE // 8, 8, TILE), axis=0)
@@ -434,14 +448,7 @@
     total_square = squares[...]
     for d in range(1, m):
         total_square += squares_in[d]
-    step = OUTER_RATE / jnp.sqrt(total_square / elements + EPSILON)
-    step = step[0:1, 0:1]
-
-    @pl.loop(0, n)
-    def _(group):
-        new_params_ref[rows_of(group), :] = (
-            params_ref[rows_of(group), :].astype(F32) - update[rows_of(group), :].astype(F32) * step
-        ).astype(BF16)
+    step_ref[...] = OUTER_RATE / jnp.sqrt(total_square / elements + EPSILON)
 
     @pl.loop(1, n)
     def _(d):
@@ -466,22 +473,23 @@
     slots = momentum.shape[1] // kept
     chunk = (n, 8, TILE)
     vmem = pl.BlockSpec(memory_space=pltpu.VMEM)
-    new_params, new_error, new_momentum = pl.pallas_call(
+    update, new_error, new_momentum, step = pl.pallas_call(
         functools.partial(kernel, n, m, rows * m * columns),
         out_shape=(
             jax.ShapeDtypeStruct((rows, columns), BF16),
             jax.ShapeDtypeStruct((rows, columns), BF16),
             jax.ShapeDtypeStruct((slots, kept), F32),
+            jax.ShapeDtypeStruct((8, 128), F32),
         ),
-        in_specs=[vmem] * 10,
-        out_specs=(vmem, vmem, vmem),
+        in_specs=[vmem] * 9,
+        out_specs=(vmem,) * 4,
         scratch_shapes=[
+            pltpu.VMEM((units, TILE, TILE), BF16),
             pltpu.VMEM((n, 16, TILE), F32),
             pltpu.VMEM((n, 16, TILE), F32),
             pltpu.VMEM(chunk, F32),
             pltpu.VMEM(chunk, F32),
             pltpu.VMEM(chunk, F32),
-            pltpu.VMEM((rows, columns), BF16),
             pltpu.VMEM((8, 128), F32),
             pltpu.VMEM((m, 8, 128), F32),
             pltpu.SemaphoreType.DMA((n,)),
@@ -500,7 +508,6 @@
     )(
         pseudo_grad[0],
         error_buf[0],
-        params,
         momentum.reshape(slots, kept),
         sel_blocks,
         sel_blocks.reshape(-1, 1),
@@ -509,6 +516,7 @@
         owner_map.reshape(n_blocks, 1),
         jnp.asarray(cosine_parts()),
     )
+    new_params = (params.astype(F32) - update.astype(F32) * step[0, 0]).astype(BF16)
     return (new_params, new_error[None], new_momentum.reshape(1, slots * kept))
 
 

time: 65.9 us -> 58.2 us (0.88)
  Pallas kernels: 51.3 us -> 44.8 us
  local copies, waits for them, and re-layouts: 12.2 us -> 8.33 us
  other arithmetic: 1.38 us -> 3.98 us
    pallas_call x1, Pallas kernels: 51.3 us -> 44.8 us  [on_device(): pl.pallas_call(functools.partial(kernel, n, m, rows * m * columns), out_s...]
    unnamed x10 -> x9, local copies, waits for them, and re-layouts: 8.81 us -> 4.46 us
    convert_element_type x0 -> x1, other arithmetic: none -> 2.59 us  [on_device(): (params.astype(F32) - update.astype(F32) * step[0, 0]).astype(BF16)]
where the time goes in v1:
time: 58.2 us; the launch traced here: 57.8 us
  Pallas kernels  44.8 us (77%)
  local copies, waits for them, and re-layouts  8.33 us (14%)
  other arithmetic  3.98 us (7%)
  between operations  0.68 us (1%)
    pallas_call x1, Pallas kernels, on_device(): pl.pallas_call(functools.partial(kernel, n, m, rows * m * columns), out_s...  44.8 us
    unnamed x9, local copies, waits for them, and re-layouts  4.46 us
    convert_element_type x1, other arithmetic, on_device(): (params.astype(F32) - update.astype(F32) * step[0, 0]).astype(BF16)  2.59 us
    unnamed x1, other arithmetic  1.38 us

profile of v1, /device:TPU:0, one launch (start us, length us, event | category | flops | bytes accessed | tf_op | source)
XLA Modules:
  0.0 57.8 jit_solution(2889037957720512952)
XLA Ops:
  0.6 0.5 broadcast.3
  1.1 1.4 %reduce.3 = f32[3072]{0:T(1024)S(1)} reduce(f32[1,3072]{1,0:T(1,128)} %param.11, f32[]{:T(128)} %broadcast.3), dimensions={0}, to_apply=%param.11.reduce_sub_computation.3 | reduce | bytes 24580 | tf_op args[3]
  2.5 0.1 reshape.27.mom_ref
  2.6 0.8 %reshape.30 = s32[64,4]{1,0:T(8,128)S(1)} reshape(s32[256]{0:T(256)} %param.14) | data formatting | bytes 2048 | tf_op jit(solution)/shard_map/reshape | solution.py:515
  3.4 0.1 copy.14
  3.5 0.1 reshape.31.owner_row_ref
  3.5 0.8 %copy.15.sel_col_ref = s32[128,1]{1,0:T(8,128)S(1)} copy(s32[128,1]{0,1:T(1,128)} %bitcast.8) | data formatting | bytes 1024 | tf_op jit(solution)/shard_map/reshape | solution.py:513
  4.3 0.9 %copy.13 = s32[256,64]{1,0:T(8,128)S(1)} copy(s32[256,64]{0,1:T(8,128)} %param.13) | data formatting | bytes 131072 | tf_op args[5]
  5.2 0.1 reshape.29.index_ref
  5.3 0.8 %copy.16.owner_col_ref = s32[256,1]{1,0:T(8,128)S(1)} copy(s32[256,1]{0,1:T(1,128)} %bitcast.12) | data formatting | bytes 2048 | tf_op jit(solution)/shard_map/reshape | solution.py:516
  6.2 0.0 copy-start
  6.2 1.0 %copy-done = bf16[4,256,256]{2,1,0:T(8,128)(2,1)S(1)} copy-done((bf16[4,256,256]{2,1,0:T(8,128)(2,1)S(1)}, bf16[4,256,256]{2,1,0:T(8,128)(2,1)}, u32[]{:S(2)}) %copy-start) | copy-done | bytes 524312
  7.2 0.0 copy-start.1
  7.2 0.7 %copy-done.1 = s32[1,128]{1,0:T(1,128)S(1)} copy-done((s32[1,128]{1,0:T(1,128)S(1)}, s32[1,128]{1,0:T(1,128)}, u32[]{:S(2)}) %copy-start.1) | copy-done | bytes 536
  7.9 0.0 copy-start.2
  7.9 44.8 %outer_step.1 = (bf16[2048,512]{1,0:T(8,128)(2,1)S(1)}, bf16[2048,512]{1,0:T(8,128)(2,1)S(1)}, f32[48,64]{1,0:T(8,128)S(1)}, f32[8,128]{1,0:T(8,128)S(1)}) custom-call(bf16[2048,512]{1,0:T(8,128)(2,1)} %bitcast.9, bf16[2048,512]{1,0:T(8,128)(2,1)} %bitcast.10, f32[48,64]{1,0:T(8,128)S(1)} %reshape.27.mom_ref, s32[1,128]{1,0:T(1,128)S(1)} %copy-done.1, ...), custom_call_target="tpu_custom_call" | custom-call | tf_op jit(solution)/shard_map/outer_step/pallas_call | solution.py:476
  52.7 0.5 slice.3
  53.2 0.0 copy-done.2
  53.2 2.6 %subtract_convert_fusion = bf16[2048,512]{1,0:T(8,128)(2,1)} fusion(bf16[2048,512]{1,0:T(8,128)(2,1)S(1)} %get-tuple-element.7, bf16[2048,512]{1,0:T(8,128)(2,1)S(1)} %copy-done.2, f32[]{:T(128)} %bitcast.5), kind=kLoop, calls=%fused_computation | loop fusion | flops 5242880 | bytes 6291460 | tf_op jit(solution)/shard_map/convert_element_type | solution.py:519
  55.8 0.7 %reshape.33 = f32[1,3072]{1,0:T(1,128)} reshape(f32[48,64]{1,0:T(8,128)S(1)} %get-tuple-element.10) | data formatting | bytes 24576 | tf_op jit(solution)/shard_map/reshape | solution.py:520
  56.5 1.3 %copy.18 = bf16[1,2048,512]{2,1,0:T(8,128)(2,1)} copy(bf16[1,2048,512]{2,1,0:T(8,128)(2,1)S(1)} %bitcast.7) | data formatting | bytes 4194304
Async XLA Ops:
  6.2 1.0 %copy-start = (bf16[4,256,256]{2,1,0:T(8,128)(2,1)S(1)}, bf16[4,256,256]{2,1,0:T(8,128)(2,1)}, u32[]{:S(2)}) copy-start(bf16[4,256,256]{2,1,0:T(8,128)(2,1)} %constant.2.clone.table_ref) | copy-start | bytes 1572868
  7.2 0.7 %copy-start.1 = (s32[1,128]{1,0:T(1,128)S(1)}, s32[1,128]{1,0:T(1,128)}, u32[]{:S(2)}) copy-start(s32[1,128]{1,0:T(1,128)} %sel_row_ref.1) | copy-start | bytes 1540
  7.9 45.4 %copy-start.2 = (bf16[2048,512]{1,0:T(8,128)(2,1)S(1)}, bf16[2048,512]{1,0:T(8,128)(2,1)}, u32[]{:S(2)}) copy-start(bf16[2048,512]{1,0:T(8,128)(2,1)} %param.10) | copy-start | bytes 6291460

commit v2 on v1

--- a/solution.py
+++ b/solution.py
@@ -127,9 +127,9 @@
     points = np.arange(64)[None, :]
     scaling = np.where(freqs == 0, np.sqrt(1.0 / 64.0), np.sqrt(2.0 / 64.0))
     cosine = scaling * np.cos(np.pi * (2.0 * points + 1.0) * freqs / 128.0)
-    diagonal = np.kron(np.eye(4), cosine).astype(np.float32)
+    cosine = cosine.astype(np.float32)
     parts = []
-    for table in (diagonal, diagonal.T):
+    for table in (np.tile(cosine, (1, 4)), np.tile(cosine.T, (1, 4))):
         high = table.astype(BF16)
         parts += [high, (table - high.astype(np.float32)).astype(BF16)]
     return np.stack(parts)
@@ -215,23 +215,31 @@
     return dot(table_ref[2], middle)
 
 
+def column_of(row):
+    extent = row.shape[1]
+    diagonal = iota((extent, extent), 0) == iota((extent, extent), 1)
+    column = jnp.sum(jnp.where(diagonal, row.astype(F32), 0.0), axis=1, keepdims=True)
+    return column.astype(jnp.int32)
+
+
 def kernel(
     n,
     m,
     elements,
-    grad_ref,
-    err_ref,
+    grad_hbm,
+    err_hbm,
     mom_ref,
-    sel_row_ref,
-    sel_col_ref,
+    sel_ref,
     index_ref,
-    owner_row_ref,
-    owner_col_ref,
-    table_ref,
+    owner_ref,
+    cosine_ref,
     update,
     new_err_ref,
     new_mom_ref,
     step_ref,
+    grad_ref,
+    err_ref,
+    table_ref,
     masks,
     early,
     early_in,
@@ -248,12 +256,19 @@
     coefs_recv,
     squares_send,
     squares_recv,
+    load_sem,
 ):
     me = lax.axis_index("island")
     shard = lax.axis_index("fsdp")
     units, width = index_ref.shape
-    slots, kept = mom_ref.shape
-    n_blocks = owner_col_ref.shape[0]
+    kept = 64
+    slots = mom_ref.shape[1] // kept
+    pairs = slots // 2
+    n_blocks = owner_ref.shape[1]
+    load_grad = pltpu.make_async_copy(grad_hbm, grad_ref, load_sem.at[0])
+    load_err = pltpu.make_async_copy(err_hbm, err_ref, load_sem.at[1])
+    load_grad.start()
+    load_err.start()
 
     def island_peer(d):
         return lax.rem(me + d, n)
@@ -269,28 +284,37 @@
             barrier, inc=1, device_id=(me, lax.rem(shard + d, m)), device_id_type=MESH
         )
 
-    in_unit = iota((units, sel_row_ref.shape[1]), 0) == lax.shift_right_logical(sel_row_ref[...], 2)
     lane_block = lax.shift_right_logical(iota((1, width), 1), 6)
-    in_lane = (sel_col_ref[...] & 3) == lane_block
+    for q in range(4):
+        keep = jnp.where(lane_block == q, 1.0, 0.0).astype(BF16)
+        for which in range(4):
+            table_ref[which, q * 64 : q * 64 + 64] = cosine_ref[which] * keep
+
+    sel_row = sel_ref[...]
+    sel_col = column_of(sel_row)
+    in_unit = iota((units, sel_row.shape[1]), 0) == lax.shift_right_logical(sel_row, 2)
+    in_lane = (sel_col & 3) == lane_block
     mask = dot(
         jnp.where(in_unit, 1.0, 0.0).astype(BF16), jnp.where(in_lane, 1.0, 0.0).astype(BF16)
     )
-    lanes = iota((1, n_blocks), 1)
-    block_row = lax.rem(lanes, units) * 4 + lax.div(lanes, units)
-    owner_row = owner_row_ref[...]
-    earlier = (owner_col_ref[...] == owner_row) & (iota((n_blocks, n_blocks), 0) < block_row)
+    owner_row = owner_ref[...]
+    earlier = (column_of(owner_row) == owner_row) & (
+        iota((n_blocks, n_blocks), 0) < iota((n_blocks, n_blocks), 1)
+    )
     slot_row = jnp.sum(jnp.where(earlier, 1, 0), axis=0, keepdims=True)
-    held = jnp.where(
-        (iota((slots, n_blocks), 0) == slot_row) & (owner_row == me), 1.0, 0.0
-    )
-    momentum = mom_ref[...]
-    previous = jnp.concatenate(
-        [
-            exact_dot(held[:, j * units : (j + 1) * units], momentum, ((0,), (0,)))
-            for j in range(4)
-        ],
-        axis=1,
-    )
+    place = iota((slots, n_blocks), 0)
+    slot_at = jnp.where(place < pairs, 2 * place, 2 * (place - pairs) + 1)
+    held = jnp.where((slot_at == slot_row) & (owner_row == me), 1.0, 0.0)
+    paired = jnp.concatenate([mom_ref[0:1, p * 128 : p * 128 + 128] for p in range(pairs)], axis=0)
+    momentum = jnp.concatenate([paired[:, :kept], paired[:, kept:]], axis=0)
+    unit_of = jnp.where(
+        iota((units, n_blocks), 0) == lax.shift_right_logical(iota((units, n_blocks), 1), 2),
+        1.0,
+        0.0,
+    )
+    in_place = (iota((n_blocks, width), 0) & 3) == lane_block
+    by_block = exact_dot(held, jnp.concatenate([momentum] * 4, axis=1), ((0,), (0,)))
+    previous = exact_dot(unit_of, jnp.where(in_place, by_block, 0.0), ((1,), (0,)))
     for q in range(n):
         early[q, 0:8] = mask[8 * q : 8 * q + 8]
         early[q, 8:16] = previous[8 * q : 8 * q + 8]
@@ -350,6 +374,9 @@
     @pl.loop(1, n)
     def _(d):
         early_copy(d).start()
+
+    load_grad.wait()
+    load_err.wait()
 
     def pick_group(group):
         positions = index_ref[units_of(group), :]
@@ -432,16 +459,17 @@
         squares_copy(d).start()
 
     everything = jnp.concatenate([coefs[q] for q in range(n)], axis=0)
-    own = jnp.zeros((slots, kept), F32)
-    for j in range(4):
-        own += exact_dot(
-            held[:, j * units : (j + 1) * units],
-            everything[:, j * kept : (j + 1) * kept],
-            ((1,), (0,)),
-        )
+    by_block = exact_dot(unit_of, everything, ((0,), (0,)))
+    wide_own = exact_dot(held, jnp.where(in_place, by_block, 0.0), ((1,), (0,)))
+    own = wide_own[:, :kept]
+    for j in range(1, 4):
+        own += wide_own[:, j * kept : (j + 1) * kept]
     live = jnp.sum(held, axis=1, keepdims=True)
     own_average = (own - (BETA_FACTOR * BETA_FACTOR) * momentum * live) / (1.0 + BETA_FACTOR)
-    new_mom_ref[...] = BETA_FACTOR * momentum + own_average
+    refreshed = BETA_FACTOR * momentum + own_average
+    refreshed = jnp.concatenate([refreshed[:pairs], refreshed[pairs:]], axis=1)
+    for p in range(pairs):
+        new_mom_ref[0:1, p * 128 : p * 128 + 128] = refreshed[p : p + 1]
 
     for d in range(1, m):
         squares_copy(d).wait_recv()
@@ -466,7 +494,7 @@
     rows, columns = params.shape
     n_blocks, kept = coef_index.shape
     units = n_blocks // 4
-    if rows != n * TILE or columns != 2 * TILE or kept != 64:
+    if rows != n * TILE or columns != 2 * TILE or kept != 64 or momentum.shape[1] % 128:
         return plain_on_device(
             pseudo_grad, error_buf, params, momentum, sel_blocks, coef_index, owner_map
         )
@@ -478,12 +506,15 @@
         out_shape=(
             jax.ShapeDtypeStruct((rows, columns), BF16),
             jax.ShapeDtypeStruct((rows, columns), BF16),
-            jax.ShapeDtypeStruct((slots, kept), F32),
+            jax.ShapeDtypeStruct((1, slots * kept), F32),
             jax.ShapeDtypeStruct((8, 128), F32),
         ),
-        in_specs=[vmem] * 9,
+        in_specs=[pl.BlockSpec(memory_space=pl.ANY)] * 2 + [vmem] * 5,
         out_specs=(vmem,) * 4,
         scratch_shapes=[
+            pltpu.VMEM((rows, columns), BF16),
+            pltpu.VMEM((rows, columns), BF16),
+            pltpu.VMEM((4, TILE, TILE), BF16),
             pltpu.VMEM((units, TILE, TILE), BF16),
             pltpu.VMEM((n, 16, TILE), F32),
             pltpu.VMEM((n, 16, TILE), F32),
@@ -500,6 +531,7 @@
             pltpu.SemaphoreType.DMA((n,)),
             pltpu.SemaphoreType.DMA((m,)),
             pltpu.SemaphoreType.DMA((m,)),
+            pltpu.SemaphoreType.DMA((2,)),
         ],
         compiler_params=pltpu.CompilerParams(
             collective_id=0, has_side_effects=True, vmem_limit_bytes=48 * 2**20
@@ -508,16 +540,14 @@
     )(
         pseudo_grad[0],
         error_buf[0],
-        momentum.reshape(slots, kept),
+        momentum,
         sel_blocks,
-        sel_blocks.reshape(-1, 1),
         coef_index.reshape(units, TILE),
-        owner_map.reshape(units, 4).T.reshape(1, n_blocks),
-        owner_map.reshape(n_blocks, 1),
+        owner_map.reshape(1, n_blocks),
         jnp.asarray(cosine_parts()),
     )
     new_params = (params.astype(F32) - update.astype(F32) * step[0, 0]).astype(BF16)
-    return (new_params, new_error[None], new_momentum.reshape(1, slots * kept))
+    return (new_params, new_error[None], new_momentum)
 
 
 def solution(mesh):

time: 58.2 us -> 52.4 us (0.900)
  Pallas kernels: 44.8 us -> 42.4 us
  local copies, waits for them, and re-layouts: 8.33 us -> 6.4 us
  other arithmetic: 3.98 us -> 2.67 us
    reshape x6 -> x0, local copies, waits for them, and re-layouts: 3.2 us -> none  [the longest x2 0.86 us: on_device(): owner_map.reshape(units, 4).T.reshape(1, n_blocks)]
    pallas_call x1, Pallas kernels: 44.8 us -> 42.4 us  [on_device(): pl.pallas_call(functools.partial(kernel, n, m, rows * m * columns), out_s...]
    unnamed x1 -> x0, other arithmetic: 1.38 us -> none
    unnamed x9 -> x13, local copies, waits for them, and re-layouts: 4.46 us -> 5.79 us
where the time goes in v2:
time: 52.4 us; the launch traced here: 52.1 us
  Pallas kernels  42.4 us (81%)
  local copies, waits for them, and re-layouts  6.4 us (12%)
  other arithmetic  2.67 us (5%)
  between operations  0.66 us (1%)
    pallas_call x1, Pallas kernels, on_device(): pl.pallas_call(functools.partial(kernel, n, m, rows * m * columns), out_s...  42.4 us
    unnamed x13, local copies, waits for them, and re-layouts  5.79 us
    convert_element_type x1, other arithmetic, on_device(): (params.astype(F32) - update.astype(F32) * step[0, 0]).astype(BF16)  2.67 us

profile of v2, /device:TPU:0, one launch (start us, length us, event | category | flops | bytes accessed | tf_op | source)
XLA Modules:
  0.0 52.1 jit_solution(9657925207763325706)
XLA Ops:
  0.6 0.9 %copy.12 = s32[256,64]{1,0:T(8,128)S(1)} copy(s32[256,64]{0,1:T(8,128)} %param.13) | data formatting | bytes 131072 | tf_op args[5]
  1.6 0.1 reshape.12.index_ref
  1.7 0.0 copy-start
  1.7 0.9 %copy-done = bf16[4,64,256]{2,1,0:T(8,128)(2,1)S(1)} copy-done((bf16[4,64,256]{2,1,0:T(8,128)(2,1)S(1)}, bf16[4,64,256]{2,1,0:T(8,128)(2,1)}, u32[]{:S(2)}) %copy-start) | copy-done | bytes 131096
  2.6 0.0 copy-start.1
  2.6 0.7 %copy-done.1 = f32[1,3072]{1,0:T(1,128)S(1)} copy-done((f32[1,3072]{1,0:T(1,128)S(1)}, f32[1,3072]{1,0:T(1,128)}, u32[]{:S(2)}) %copy-start.1) | copy-done | bytes 12312
  3.3 0.0 copy-start.2
  3.3 0.7 %copy-done.2 = s32[256]{0:T(256)S(1)} copy-done((s32[256]{0:T(256)S(1)}, s32[256]{0:T(256)}, u32[]{:S(2)}) %copy-start.2) | copy-done | bytes 1048
  4.0 0.0 copy-start.3
  4.0 0.7 %copy-done.3 = s32[1,128]{1,0:T(1,128)S(1)} copy-done((s32[1,128]{1,0:T(1,128)S(1)}, s32[1,128]{1,0:T(1,128)}, u32[]{:S(2)}) %copy-start.3) | copy-done | bytes 536
  4.6 0.0 copy-start.4
  4.6 42.4 %outer_step.1 = (bf16[2048,512]{1,0:T(8,128)(2,1)S(1)}, bf16[2048,512]{1,0:T(8,128)(2,1)S(1)}, f32[1,3072]{1,0:T(1,128)S(1)}, f32[8,128]{1,0:T(8,128)S(1)}) custom-call(bf16[2048,512]{1,0:T(8,128)(2,1)} %bitcast.7, bf16[2048,512]{1,0:T(8,128)(2,1)} %bitcast.8, f32[1,3072]{1,0:T(1,128)S(1)} %copy-done.1, s32[1,128]{1,0:T(1,128)S(1)} %copy-done.3, ...), custom_call_target="tpu_custom_call" | custom-call | tf_op jit(solution)/shard_map/outer_step/pallas_call | solution.py:504
  47.0 0.5 slice.3
  47.5 0.0 copy-done.4
  47.5 2.7 %subtract_convert_fusion = bf16[2048,512]{1,0:T(8,128)(2,1)} fusion(bf16[2048,512]{1,0:T(8,128)(2,1)S(1)} %get-tuple-element.7, bf16[2048,512]{1,0:T(8,128)(2,1)S(1)} %copy-done.4, f32[]{:T(128)} %bitcast.3), kind=kLoop, calls=%fused_computation | loop fusion | flops 5242880 | bytes 6291460 | tf_op jit(solution)/shard_map/convert_element_type | solution.py:549
  50.2 1.3 %copy.15 = bf16[1,2048,512]{2,1,0:T(8,128)(2,1)} copy(bf16[1,2048,512]{2,1,0:T(8,128)(2,1)S(1)} %bitcast.5) | data formatting | bytes 4194304
  51.5 0.6 %copy.16 = f32[1,3072]{1,0:T(1,128)} copy(f32[1,3072]{1,0:T(1,128)S(1)} %get-tuple-element.16) | data formatting | bytes 24576
Async XLA Ops:
  1.7 0.9 %copy-start = (bf16[4,64,256]{2,1,0:T(8,128)(2,1)S(1)}, bf16[4,64,256]{2,1,0:T(8,128)(2,1)}, u32[]{:S(2)}) copy-start(bf16[4,64,256]{2,1,0:T(8,128)(2,1)} %constant.2.clone.cosine_ref) | copy-start | bytes 393220
  2.6 0.7 %copy-start.1 = (f32[1,3072]{1,0:T(1,128)S(1)}, f32[1,3072]{1,0:T(1,128)}, u32[]{:S(2)}) copy-start(f32[1,3072]{1,0:T(1,128)} %mom_ref.1) | copy-start | bytes 36868
  3.3 0.7 %copy-start.2 = (s32[256]{0:T(256)S(1)}, s32[256]{0:T(256)}, u32[]{:S(2)}) copy-start(s32[256]{0:T(256)} %param.14) | copy-start | bytes 3076
  4.0 0.7 %copy-start.3 = (s32[1,128]{1,0:T(1,128)S(1)}, s32[1,128]{1,0:T(1,128)}, u32[]{:S(2)}) copy-start(s32[1,128]{1,0:T(1,128)} %sel_ref.1) | copy-start | bytes 1540
  4.6 42.9 %copy-start.4 = (bf16[2048,512]{1,0:T(8,128)(2,1)S(1)}, bf16[2048,512]{1,0:T(8,128)(2,1)}, u32[]{:S(2)}) copy-start(bf16[2048,512]{1,0:T(8,128)(2,1)} %param.10) | copy-start | bytes 6291460

commit v3 on v2

--- a/solution.py
+++ b/solution.py
@@ -409,7 +409,7 @@
                 summed(group, half) - rebuilt
             ).astype(BF16)
 
-    @pl.loop(0, n // 2)
+    @pl.loop(0, 3 * n // 8)
     def _(group):
         error_group(group)
 
@@ -432,7 +432,7 @@
     def _(d):
         coefs_copy(d, me).start()
 
-    @pl.loop(n // 2, n)
+    @pl.loop(3 * n // 8, 3 * n // 4)
     def _(group):
         error_group(group)
 
@@ -471,12 +471,17 @@
     for p in range(pairs):
         new_mom_ref[0:1, p * 128 : p * 128 + 128] = refreshed[p : p + 1]
 
+    @pl.loop(3 * n // 4, n)
+    def _(group):
+        error_group(group)
+
     for d in range(1, m):
         squares_copy(d).wait_recv()
     total_square = squares[...]
     for d in range(1, m):
         total_square += squares_in[d]
-    step_ref[...] = OUTER_RATE / jnp.sqrt(total_square / elements + EPSILON)
+    step = OUTER_RATE / jnp.sqrt(total_square / elements + EPSILON)
+    step_ref[...] = step[0:1, 0:1]
 
     @pl.loop(1, n)
     def _(d):
@@ -507,7 +512,7 @@
             jax.ShapeDtypeStruct((rows, columns), BF16),
             jax.ShapeDtypeStruct((rows, columns), BF16),
             jax.ShapeDtypeStruct((1, slots * kept), F32),
-            jax.ShapeDtypeStruct((8, 128), F32),
+            jax.ShapeDtypeStruct((1, 1), F32),
         ),
         in_specs=[pl.BlockSpec(memory_space=pl.ANY)] * 2 + [vmem] * 5,
         out_specs=(vmem,) * 4,
@@ -546,7 +551,7 @@
         owner_map.reshape(1, n_blocks),
         jnp.asarray(cosine_parts()),
     )
-    new_params = (params.astype(F32) - update.astype(F32) * step[0, 0]).astype(BF16)
+    new_params = (params.astype(F32) - update.astype(F32) * step).astype(BF16)
     return (new_params, new_error[None], new_momentum)
 
 

time: 52.4 us -> 50.3 us (0.960)
  Pallas kernels: 42.4 us -> 40.9 us
    pallas_call x1, Pallas kernels: 42.4 us -> 40.9 us  [on_device(): pl.pallas_call(functools.partial(kernel, n, m, rows * m * columns), out_s...]
where the time goes in v3:
time: 50.3 us; the launch traced here: 50.1 us
  Pallas kernels  40.9 us (81%)
  local copies, waits for them, and re-layouts  5.89 us (12%)
  other arithmetic  2.61 us (5%)
  between operations  0.66 us (1%)
    pallas_call x1, Pallas kernels, on_device(): pl.pallas_call(functools.partial(kernel, n, m, rows * m * columns), out_s...  40.9 us
    unnamed x13, local copies, waits for them, and re-layouts  5.79 us
    convert_element_type x1, other arithmetic, on_device(): new_params = (params.astype(F32) - update.astype(F32) * step).astype(BF16)  2.61 us

profile of v3, /device:TPU:0, one launch (start us, length us, event | category | flops | bytes accessed | tf_op | source)
XLA Modules:
  0.0 50.1 jit_solution(12940129196987719071)
XLA Ops:
  0.6 0.9 %copy.12 = s32[256,64]{1,0:T(8,128)S(1)} copy(s32[256,64]{0,1:T(8,128)} %param.13) | data formatting | bytes 131072 | tf_op args[5]
  1.6 0.1 reshape.12.index_ref
  1.7 0.0 copy-start
  1.7 0.9 %copy-done = bf16[4,64,256]{2,1,0:T(8,128)(2,1)S(1)} copy-done((bf16[4,64,256]{2,1,0:T(8,128)(2,1)S(1)}, bf16[4,64,256]{2,1,0:T(8,128)(2,1)}, u32[]{:S(2)}) %copy-start) | copy-done | bytes 131096
  2.6 0.0 copy-start.1
  2.6 0.7 %copy-done.1 = f32[1,3072]{1,0:T(1,128)S(1)} copy-done((f32[1,3072]{1,0:T(1,128)S(1)}, f32[1,3072]{1,0:T(1,128)}, u32[]{:S(2)}) %copy-start.1) | copy-done | bytes 12312
  3.3 0.0 copy-start.2
  3.3 0.7 %copy-done.2 = s32[256]{0:T(256)S(1)} copy-done((s32[256]{0:T(256)S(1)}, s32[256]{0:T(256)}, u32[]{:S(2)}) %copy-start.2) | copy-done | bytes 1048
  4.0 0.0 copy-start.3
  4.0 0.7 %copy-done.3 = s32[1,128]{1,0:T(1,128)S(1)} copy-done((s32[1,128]{1,0:T(1,128)S(1)}, s32[1,128]{1,0:T(1,128)}, u32[]{:S(2)}) %copy-start.3) | copy-done | bytes 536
  4.6 0.0 copy-start.4
  4.6 40.9 %outer_step.1 = (bf16[2048,512]{1,0:T(8,128)(2,1)S(1)}, bf16[2048,512]{1,0:T(8,128)(2,1)S(1)}, f32[1,3072]{1,0:T(1,128)S(1)}, f32[1,1]{1,0:T(1,128)}) custom-call(bf16[2048,512]{1,0:T(8,128)(2,1)} %bitcast.7, bf16[2048,512]{1,0:T(8,128)(2,1)} %bitcast.8, f32[1,3072]{1,0:T(1,128)S(1)} %copy-done.1, s32[1,128]{1,0:T(1,128)S(1)} %copy-done.3, ...), custom_call_target="tpu_custom_call" | custom-call | tf_op jit(solution)/shard_map/outer_step/pallas_call | solution.py:509
  45.5 0.0 copy-done.4
  45.5 2.6 %subtract_convert_fusion = bf16[2048,512]{1,0:T(8,128)(2,1)} fusion(bf16[2048,512]{1,0:T(8,128)(2,1)S(1)} %get-tuple-element.7, bf16[2048,512]{1,0:T(8,128)(2,1)S(1)} %copy-done.4, f32[]{:T(128)} %bitcast.3), kind=kLoop, calls=%fused_computation | loop fusion | flops 5242880 | bytes 6291460 | tf_op jit(solution)/shard_map/convert_element_type | solution.py:554
  48.2 1.3 %copy.15 = bf16[1,2048,512]{2,1,0:T(8,128)(2,1)} copy(bf16[1,2048,512]{2,1,0:T(8,128)(2,1)S(1)} %bitcast.5) | data formatting | bytes 4194304
  49.5 0.6 %copy.16 = f32[1,3072]{1,0:T(1,128)} copy(f32[1,3072]{1,0:T(1,128)S(1)} %get-tuple-element.16) | data formatting | bytes 24576
Async XLA Ops:
  1.7 0.9 %copy-start = (bf16[4,64,256]{2,1,0:T(8,128)(2,1)S(1)}, bf16[4,64,256]{2,1,0:T(8,128)(2,1)}, u32[]{:S(2)}) copy-start(bf16[4,64,256]{2,1,0:T(8,128)(2,1)} %constant.2.clone.cosine_ref) | copy-start | bytes 393220
  2.6 0.7 %copy-start.1 = (f32[1,3072]{1,0:T(1,128)S(1)}, f32[1,3072]{1,0:T(1,128)}, u32[]{:S(2)}) copy-start(f32[1,3072]{1,0:T(1,128)} %mom_ref.1) | copy-start | bytes 36868
  3.3 0.7 %copy-start.2 = (s32[256]{0:T(256)S(1)}, s32[256]{0:T(256)}, u32[]{:S(2)}) copy-start(s32[256]{0:T(256)} %param.14) | copy-start | bytes 3076
  4.0 0.7 %copy-start.3 = (s32[1,128]{1,0:T(1,128)S(1)}, s32[1,128]{1,0:T(1,128)}, u32[]{:S(2)}) copy-start(s32[1,128]{1,0:T(1,128)} %sel_ref.1) | copy-start | bytes 1540
  4.6 40.9 %copy-start.4 = (bf16[2048,512]{1,0:T(8,128)(2,1)S(1)}, bf16[2048,512]{1,0:T(8,128)(2,1)}, u32[]{:S(2)}) copy-start(bf16[2048,512]{1,0:T(8,128)(2,1)} %param.10) | copy-start | bytes 6291460
